TPU v7x, 256 devices: a whole 4x4x8 slice. The times are simulated.
256 devices in a mesh: seq: 8 (over y, core), ep: 32 (over x, z).
Axes of the slice: x: 4, y: 4, z: 8, core: 2. Of those that a mesh axis runs over, the one named last changes fastest.
Arguments:
- entering: bfloat16 [32, 32, 7168], P('ep', 'seq'), may hold values from -6 to 6
- moe_gain: float32 [7168], replicated, may hold values from 0.1 to 1.9
- expert_ids: int32 [32, 32, 8], P('ep'), may hold values from 0 to 31, all different within a row; in each aligned block of 4 rows (0 to 3, 4 to 7, ..., all dimensions but the last counted through in order) at most 2 rows name the same one
- gate_weights: float32 [32, 32, 8], P('ep'), may hold values from 0.05 to 0.5
- w_gate: bfloat16 [32, 7168, 2048], P('ep', None, 'seq'), may hold values from -0.0625 to 0.0625
- w_up: bfloat16 [32, 7168, 2048], P('ep', None, 'seq'), may hold values from -0.0625 to 0.0625
- w_down: bfloat16 [32, 2048, 7168], P('ep', 'seq'), may hold values from -0.125 to 0.125
- w_latent: bfloat16 [7168, 512], P('seq'), may hold values from -0.0625 to 0.0625
- w_rope: bfloat16 [64, 7168], P(None, 'seq'), may hold values from -0.0625 to 0.0625
- latent_gain: float32 [512], replicated, may hold values from 0.1 to 1.9
- prefix_len: int32 [32], P('ep'), may hold values from 128 to 1024, as said below
- cache_latent: bfloat16 [32, 1024, 512], P('ep', 'seq'), may hold values from -4 to 4
- cache_rope: bfloat16 [32, 64, 1024], P('ep', None, 'seq'), may hold values from -4 to 4
- query_latent: bfloat16 [32, 32, 65536], P('ep', 'seq'), may hold values from -7 to 7
- query_rope: bfloat16 [32, 32, 8192], P('ep', 'seq'), may hold values from -32 to 32
Outputs:
- layer_out: bfloat16 [32, 32, 7168], P('ep', None, 'seq')
- attention: bfloat16 [32, 32, 65536], P('ep', 'seq')
Inputs may be any that keep to these rules, and one draw needn't show every extreme that they name: `expert_ids`: in each aligned block of 4 rows (one document's new tokens on one index of seq) no expert is named by more than 2 tokens, and in some blocks one is named by exactly 2. Each token names 8 different experts. `prefix_len`: some document has all 1024 positions cached.
All inputs are finite; a program needn't handle non-finite values.
Results may differ from a plain program's by a relative error of at most 0.018.
Values may be sent and summed in bfloat16 or wider, within the bound.
A program may use at most 128 MiB of HBM per device.

v0:
```python
import jax
import jax.numpy as jnp
from jax import lax
from jax.sharding import PartitionSpec as P

softmax_scale = 192 ** (-0.5)
rope_base = 10000.0


def rms_rows(values, gain):
    mean_sq = jnp.mean(values * values, axis=-1, keepdims=True)
    return values * lax.rsqrt(mean_sq + 1e-06) * gain


def rotate_pairs(values, positions):
    half = values.shape[-1] // 2
    steps = jnp.arange(half, dtype=jnp.float32) * 2.0 / values.shape[-1]
    freqs = rope_base ** (-steps)
    angle = positions.astype(jnp.float32)[:, None] * freqs[None, :]
    first = values[:, :half]
    second = values[:, half:]
    cosine = jnp.cos(angle)
    sine = jnp.sin(angle)
    return jnp.concatenate(
        [first * cosine - second * sine, second * cosine + first * sine], axis=-1
    )


def score_block(query_lat, query_rot, key_lat, key_rot_cols):
    lat_part = jnp.dot(query_lat, key_lat.T, preferred_element_type=jnp.float32)
    rot_part = jnp.dot(query_rot, key_rot_cols, preferred_element_type=jnp.float32)
    return (lat_part + rot_part) * softmax_scale


def block_slots(routes, experts, capacity):
    same = (routes[:, :, None, None] == routes[None, None, :, :]).any(axis=3)
    order = jnp.arange(routes.shape[0], dtype=jnp.int32)
    earlier = order[None, :] < order[:, None]
    slots = jnp.sum((same & earlier[:, None, :]).astype(jnp.int32), axis=2)
    return routes * capacity + slots


def expert_terms(rows, gate_matrix, up_matrix, down_matrix):
    gate = jnp.dot(rows, gate_matrix, preferred_element_type=jnp.float32)
    upper = jnp.dot(rows, up_matrix, preferred_element_type=jnp.float32)
    hidden = (jax.nn.silu(gate) * upper).astype(jnp.bfloat16)
    return jnp.dot(hidden, down_matrix, preferred_element_type=jnp.float32)


def local(
    entering,
    moe_gain,
    expert_ids,
    gate_weights,
    w_gate,
    w_up,
    w_down,
    w_latent,
    w_rope,
    latent_gain,
    prefix_len,
    cache_latent,
    cache_rope,
    query_latent,
    query_rope,
):
    seq_count = lax.axis_size("seq")
    seq_place = lax.axis_index("seq")
    experts = lax.axis_size("ep")
    own_entering = entering[0]
    new_dev, width = own_entering.shape
    new = new_dev * seq_count
    capacity = 2
    prefix = prefix_len[0]
    heads = query_latent.shape[2] // cache_latent.shape[2]
    lat_width = cache_latent.shape[2]
    rot_width = cache_rope.shape[1]
    routes = lax.dynamic_slice_in_dim(expert_ids[0], seq_place * new_dev, new_dev, 0)
    gates = lax.dynamic_slice_in_dim(gate_weights[0], seq_place * new_dev, new_dev, 0)
    normed = rms_rows(own_entering.astype(jnp.float32), moe_gain).astype(jnp.bfloat16)
    targets = block_slots(routes, experts, capacity)
    total_slots = experts * capacity
    hits = targets[:, :, None] == jnp.arange(total_slots, dtype=jnp.int32)[None, None, :]
    placement = jnp.any(hits, axis=1).astype(jnp.bfloat16)
    gate_rows = jnp.sum(jnp.where(hits, gates[:, :, None], 0.0), axis=1)
    outgoing = jnp.dot(placement.T, normed, preferred_element_type=jnp.float32)
    outgoing = outgoing.astype(jnp.bfloat16).reshape(experts, capacity, width)
    arrived = lax.all_to_all(outgoing, "ep", split_axis=0, concat_axis=0, tiled=True)
    rows = lax.all_gather(arrived.reshape(total_slots, width), "seq", axis=0, tiled=True)
    older_lat = lax.all_gather(cache_latent[0], "seq", axis=0, tiled=True)
    older_rot = lax.all_gather(cache_rope[0], "seq", axis=1, tiled=True)
    query_lat = query_latent[0].reshape(new_dev * heads, lat_width)
    query_rot = query_rope[0].reshape(new_dev * heads, rot_width)
    older = score_block(query_lat, query_rot, older_lat, older_rot)
    cache_ok = (jnp.arange(older_lat.shape[0], dtype=jnp.int32) < prefix)[None, :]
    older = jnp.where(cache_ok, older, -jnp.inf)
    older_high = jnp.max(older, axis=1)
    older_weights = jnp.exp(older - older_high[:, None])
    older_total = jnp.sum(older_weights, axis=1)
    older_sum = jnp.dot(
        older_weights.astype(jnp.bfloat16), older_lat, preferred_element_type=jnp.float32
    )
    terms = expert_terms(rows, w_gate[0], w_up[0], w_down[0]).astype(jnp.bfloat16)
    summed = lax.psum_scatter(terms, "seq", scatter_dimension=0, tiled=True)
    summed = summed.reshape(experts, capacity, width)
    returned = lax.all_to_all(summed, "ep", split_axis=0, concat_axis=0, tiled=True)
    weighted = jnp.dot(
        gate_rows,
        returned.reshape(total_slots, width).astype(jnp.float32),
        precision=lax.Precision.HIGHEST,
    )
    layer_own = (own_entering.astype(jnp.float32) + weighted).astype(jnp.bfloat16)
    layer = lax.all_to_all(layer_own, "seq", split_axis=1, concat_axis=0, tiled=True)
    latent_part = jnp.dot(layer, w_latent, preferred_element_type=jnp.float32)
    rope_part = lax.dot_general(
        layer, w_rope, (((1,), (1,)), ((), ())), preferred_element_type=jnp.float32
    )
    raw = lax.psum(jnp.concatenate([latent_part, rope_part], axis=1), "seq")
    fresh_lat = rms_rows(raw[:, :lat_width], latent_gain).astype(jnp.bfloat16)
    positions = prefix + jnp.arange(new, dtype=jnp.int32)
    fresh_rot = rotate_pairs(raw[:, lat_width:], positions).astype(jnp.bfloat16)
    fresh = score_block(query_lat, query_rot, fresh_lat, fresh_rot.T)
    query_place = seq_place * new_dev + jnp.arange(new_dev * heads, dtype=jnp.int32) // heads
    fresh_ok = jnp.arange(new, dtype=jnp.int32)[None, :] <= query_place[:, None]
    fresh = jnp.where(fresh_ok, fresh, -jnp.inf)
    highest = jnp.maximum(older_high, jnp.max(fresh, axis=1))
    scale = jnp.exp(older_high - highest)
    fresh_weights = jnp.exp(fresh - highest[:, None])
    total = older_total * scale + jnp.sum(fresh_weights, axis=1)
    gathered = older_sum * scale[:, None] + jnp.dot(
        fresh_weights.astype(jnp.bfloat16), fresh_lat, preferred_element_type=jnp.float32
    )
    output = (gathered / total[:, None]).astype(jnp.bfloat16).reshape(new_dev, heads * lat_width)
    return (layer[None], output[None])


def solution(mesh):
    placed = (
        P("ep", "seq", None),
        P(),
        P("ep", None, None),
        P("ep", None, None),
        P("ep", None, "seq"),
        P("ep", None, "seq"),
        P("ep", "seq", None),
        P("seq", None),
        P(None, "seq"),
        P(),
        P("ep"),
        P("ep", "seq", None),
        P("ep", None, "seq"),
        P("ep", "seq", None),
        P("ep", "seq", None),
    )
    return jax.shard_map(
        local,
        mesh=mesh,
        in_specs=placed,
        out_specs=(P("ep", None, "seq"), P("ep", "seq", None)),
        check_vma=False,
    )
```

profile of v0, /device:TPU:1, one launch (start us, length us, event | category | flops | bytes accessed | tf_op | source)
XLA Modules:
  0.0 291.2 jit_solution(7209616721143365374)
XLA Ops:
  7.2 0.0 copy-start
  7.2 0.0 all-gather.5.cloned.1.call-start
  7.2 0.8 constant_dynamic-slice_fusion.1
  8.1 0.1 copy.23
  8.2 0.4 compare_reduce_fusion
  8.6 0.1 convert_reduce_fusion
  8.7 0.1 fusion.47
  8.8 1.0 fusion.28
  9.8 1.3 convolution_convert_fusion.1
  11.1 0.3 reshape.118
  11.4 33.6 %all_to_all.29 = bf16[32,2,7168]{2,1,0:T(2,128)(2,1)S(1)} all-to-all(bf16[32,2,7168]{2,1,0:T(2,128)(2,1)S(1)} %reshape.118), channel_id=1, replica_groups=mesh['seq'=8,'ep'=32] {'ep'}, dimensions={0} | all-to-all | bytes 1835008 | tf_op jit(solution)/shard_map/all_to_all | solution.py:88
  45.0 1.3 reshape.119
  46.3 0.0 all-gather.5.cloned.1.call-update
  46.3 0.0 reduce-scatter.2.cloned.1.call-start
  46.4 49.3 %all-gather.5.cloned.1.call-done = bf16[512,7168]{1,0:T(8,128)(2,1)} async-done(((bf16[64,7168]{1,0:T(8,128)(2,1)}), bf16[512,7168]{1,0:T(8,128)(2,1)}) %all-gather.5.cloned.1.call-update) | async-done | bytes 7340048 | tf_op jit(solution)/shard_map/all_gather | solution.py:89
  95.7 6.2 %fusion.4 = f32[512,256]{1,0:T(8,128)S(1)} fusion(bf16[512,7168]{1,0:T(8,128)(2,1)} %all-gather.5.cloned.1.call-done, bf16[1,7168,256]{2,1,0:T(8,128)(2,1)} %param.19), kind=kOutput, calls=%fused_computation.7 | convolution fusion | flops 1879048192 | bytes 11534336 | tf_op jit(solution)/shard_map/dot_general | solution.py:44
  101.9 16.0 %convolution_convert_fusion = bf16[512,7168]{1,0:T(8,128)(2,1)} fusion(bf16[1,256,7168]{2,1,0:T(8,128)(2,1)} %param.21, bf16[512,7168]{1,0:T(8,128)(2,1)} %all-gather.5.cloned.1.call-done, bf16[1,7168,256]{2,1,0:T(8,128)(2,1)} %param.20, f32[512,256]{1,0:T(8,128)S(1)} %fusion.4), kind=kOutput, calls=%fused_computation | convolution fusion | flops 3762552832 | bytes 22544384 | tf_op jit(solution)/shard_map/dot_general | solution.py:47
  117.9 0.0 reduce-scatter.2.cloned.1.call-update
  117.9 0.0 copy-start.7
  117.9 0.0 copy-start.5
  117.9 0.0 copy-start.2
  118.0 0.0 copy-start.6
  118.0 49.3 %reduce-scatter.2.cloned.1.call-done = bf16[64,7168]{1,0:T(8,128)(2,1)} async-done(((bf16[512,7168]{1,0:T(8,128)(2,1)}), bf16[64,7168]{1,0:T(8,128)(2,1)}) %reduce-scatter.2.cloned.1.call-update) | async-done | bytes 917520 | tf_op jit(solution)/shard_map/reduce_scatter | solution.py:104
  167.2 3.1 %reshape.120 = bf16[32,2,7168]{2,1,0:T(2,128)(2,1)} reshape(bf16[64,7168]{1,0:T(8,128)(2,1)} %reduce-scatter.2.cloned.1.call-done) | data formatting | bytes 1835008 | tf_op jit(solution)/shard_map/reshape | solution.py:105
  170.3 9.7 %all-to-all-start.1 = ((bf16[32,2,7168]{2,1,0:T(2,128)(2,1)}), bf16[32,2,7168]{2,1,0:T(2,128)(2,1)S(1)}, u32[]{:S(2)}, u32[]{:S(2)}) async-start(bf16[32,2,7168]{2,1,0:T(2,128)(2,1)} %reshape.120), calls=%async_computation.2 | async-start | bytes 1835008 | tf_op jit(solution)/shard_map/all_to_all | solution.py:106
  180.0 0.2 all-gather.7.cloned.1.call-start
  180.2 0.5 all-gather.7.cloned.1.call-update
  180.7 0.0 copy-done.7
  180.7 0.1 constant_dynamic-slice_fusion
  180.8 0.1 copy.24
  180.9 0.0 copy-done.5
  180.9 0.2 reshape_squeeze.7
  181.1 0.0 copy-start.1
  181.1 0.4 reshape_squeeze.6
  182.2 12.7 %all-gather.1 = bf16[1,64,1024]{2,1,0:T(8,128)(2,1)S(1)} all-gather(bf16[1,64,128]{2,1,0:T(8,128)(2,1)S(1)} %copy-done.6), channel_id=3, replica_groups=mesh['seq'=8,'ep'=32] {'seq'}, dimensions={2}, use_global_device_ids=true | all-gather | bytes 147456 | tf_op jit(solution)/shard_map/all_gather | solution.py:91
  194.8 0.6 negate_power_fusion
  195.4 0.5 add_convert_fusion
  196.0 0.1 select_reduce_fusion
  196.1 1.8 fusion.26
  197.8 4.2 %all-to-all-done.1 = bf16[32,2,7168]{2,1,0:T(2,128)(2,1)S(1)} async-done(((bf16[32,2,7168]{2,1,0:T(2,128)(2,1)}), bf16[32,2,7168]{2,1,0:T(2,128)(2,1)S(1)}, u32[]{:S(2)}, u32[]{:S(2)}) %all-to-all-start.1) | async-done | bytes 917536 | tf_op jit(solution)/shard_map/all_to_all | solution.py:106
  202.0 0.3 reshape.121
  202.3 0.0 copy-done.3
  202.4 1.1 fusion
  203.5 8.9 %all-to-all-start.2 = ((bf16[4,8,896]{2,0,1:T(4,128)(2,1)}), bf16[4,8,896]{2,0,1:T(4,128)(2,1)}, u32[]{:S(2)}, u32[]{:S(2)}) async-start(bf16[4,8,896]{2,0,1:T(4,128)(2,1)} %bitcast.7), calls=%async_computation.3 | async-start | bytes 114688 | tf_op jit(solution)/shard_map/all_to_all | solution.py:113
  212.4 0.0 all-gather.7.cloned.1.call-done
  212.4 2.8 fusion.58
  215.2 2.1 all-to-all-done.2
  217.3 1.5 all_to_all.25
  218.8 1.1 fusion.61
  219.8 0.0 copy-done
  219.9 1.1 fusion.60
  220.9 0.7 pad_maximum_fusion
  221.6 0.0 all-reduce.2.cloned.1.call-update
  221.6 0.5 fusion.6
  222.1 1.5 broadcast_in_dim.34
  223.5 53.4 %all-reduce.2.cloned.1.call-done = f32[32,576]{1,0:T(8,128)} async-done(((f32[32,576]{1,0:T(8,128)}), f32[32,576]{1,0:T(8,128)}) %all-reduce.2.cloned.1.call-update) | async-done | bytes 73744 | tf_op jit(solution)/shard_map/psum | solution.py:118
  276.9 1.0 multiply_reduce_fusion
  278.0 1.1 fusion.57
  279.0 1.0 fusion.44
  280.0 1.1 fusion.59
  281.2 2.0 convolution_multiply_fusion
  283.2 0.0 copy-done.4
  283.2 0.3 fusion.9
  283.5 1.2 broadcast_in_dim_reshape.3
  (17 shorter events, 0.1 us)
Async XLA Ops:
  7.2 212.7 %copy-start = (bf16[896,512]{1,0:T(8,128)(2,1)S(1)}, bf16[896,512]{1,0:T(8,128)(2,1)}, u32[]{:S(2)}) copy-start(bf16[896,512]{1,0:T(8,128)(2,1)} %param.22) | copy-start | bytes 2752516
  7.2 88.5 %all-gather.5.cloned.1.call-start = ((), (), s32[]{:S(2)}) async-start(), calls=%async_computation.4 | async-start | bytes 8257536 | tf_op jit(solution)/shard_map/all_gather | solution.py:89
  46.3 120.9 %reduce-scatter.2.cloned.1.call-start = ((), (), s32[]{:S(2)}) async-start(), calls=%async_computation.5 | async-start | bytes 8257536 | tf_op jit(solution)/shard_map/reduce_scatter | solution.py:104
  117.9 62.8 %copy-start.7 = (f32[1,32,8]{1,2,0:T(8,128)S(1)}, f32[1,32,8]{1,2,0:T(8,128)}, u32[]{:S(2)}) copy-start(f32[1,32,8]{1,2,0:T(8,128)} %param.18) | copy-start | bytes 3076
  117.9 63.0 %copy-start.5 = (bf16[1,4,8192]{2,1,0:T(4,128)(2,1)S(1)}, bf16[1,4,8192]{2,1,0:T(4,128)(2,1)}, u32[]{:S(2)}) copy-start(bf16[1,4,8192]{2,1,0:T(4,128)(2,1)} %param.29) | copy-start | bytes 196612
  117.9 63.1 %copy-start.2 = (bf16[1,4,65536]{2,1,0:T(4,128)(2,1)S(1)}, bf16[1,4,65536]{2,1,0:T(4,128)(2,1)}, u32[]{:S(2)}) copy-start(bf16[1,4,65536]{2,1,0:T(4,128)(2,1)} %param.28) | copy-start | bytes 1572868
  118.0 64.2 %copy-start.6 = (bf16[1,64,128]{2,1,0:T(8,128)(2,1)S(1)}, bf16[1,64,128]{2,1,0:T(8,128)(2,1)}, u32[]{:S(2)}) copy-start(bf16[1,64,128]{2,1,0:T(8,128)(2,1)} %param.27) | copy-start | bytes 49156
  170.3 32.1 %copy-start.3 = (bf16[1,4,7168]{2,1,0:T(4,128)(2,1)S(1)}, bf16[1,4,7168]{2,1,0:T(4,128)(2,1)}, u32[]{:S(2)}) copy-start(bf16[1,4,7168]{2,1,0:T(4,128)(2,1)} %param.15) | copy-start | bytes 172036
  170.3 31.7 %all-to-all-start.1 = ((bf16[32,2,7168]{2,1,0:T(2,128)(2,1)}), bf16[32,2,7168]{2,1,0:T(2,128)(2,1)S(1)}, u32[]{:S(2)}, u32[]{:S(2)}) async-start(bf16[32,2,7168]{2,1,0:T(2,128)(2,1)} %reshape.120), calls=%async_computation.2 | async-start | bytes 1835008 | tf_op jit(solution)/shard_map/all_to_all | solution.py:106
  180.0 32.4 %all-gather.7.cloned.1.call-start = ((), (), s32[]{:S(2)}) async-start(), calls=%async_computation.7 | async-start | bytes 1179648 | tf_op jit(solution)/shard_map/all_gather | solution.py:90
  181.1 16.8 %copy-start.1 = (bf16[512,64]{1,0:T(8,128)(2,1)}, bf16[512,64]{1,0:T(8,128)(2,1)S(1)}, u32[]{:S(2)}) copy-start(bf16[512,64]{1,0:T(8,128)(2,1)S(1)} %reshape_squeeze.7) | copy-start | bytes 196612
  203.5 13.8 %all-to-all-start.2 = ((bf16[4,8,896]{2,0,1:T(4,128)(2,1)}), bf16[4,8,896]{2,0,1:T(4,128)(2,1)}, u32[]{:S(2)}, u32[]{:S(2)}) async-start(bf16[4,8,896]{2,0,1:T(4,128)(2,1)} %bitcast.7), calls=%async_computation.3 | async-start | bytes 114688 | tf_op jit(solution)/shard_map/all_to_all | solution.py:113
  212.4 65.6 %copy-start.8 = (f32[512]{0:T(512)S(1)}, f32[512]{0:T(512)}, u32[]{:S(2)}) copy-start(f32[512]{0:T(512)} %param.24) | copy-start | bytes 6148
  212.4 64.5 %all-reduce.2.cloned.1.call-start = ((), (), s32[]{:S(2)}) async-start(), calls=%async_computation.6 | async-start | bytes 163840 | tf_op jit(solution)/shard_map/psum | solution.py:118
  276.9 6.3 %copy-start.4 = (f32[32,576]{1,0:T(8,128)S(1)}, f32[32,576]{1,0:T(8,128)}, u32[]{:S(2)}) copy-start(f32[32,576]{1,0:T(8,128)} %all-reduce.2.cloned.1.call-done) | copy-start | bytes 221188
Sparse Core Ops, SparseCore 0:
  46.5 49.1 all-gather.4
  118.0 49.1 reduce-scatter.1
  182.7 26.2 all-gather.6
  221.7 55.1 all-reduce.1
where the time goes:
time: 292 us; the launch traced here: 291 us
  waiting for transfers between devices  159 us (54%)
  blocking collectives  46.3 us (16%)
  matrix products  35.8 us (12%)
  starting transfers between devices  18.9 us (6%)
  between operations  14.6 us (5%)
  local copies, waits for them, and re-layouts  10.8 us (4%)
  other arithmetic  6.02 us (2%)
    psum x1, waiting for transfers between devices, local(): raw = lax.psum(jnp.concatenate([latent_part, rope_part], axis=1), 'seq')  53.4 us
    all_gather x1, waiting for transfers between devices, local(): lax.all_gather(arrived.reshape(total_slots, width), 'seq', axis=0, tiled=...  49.3 us
    reduce_scatter x1, waiting for transfers between devices, local(): summed = lax.psum_scatter(terms, 'seq', scatter_dimension=0, tiled=True)  49.3 us
    all_to_all x1, blocking collectives, local(): lax.all_to_all(outgoing, 'ep', split_axis=0, concat_axis=0, tiled=True)  33.6 us
    dot_general x1, matrix products, expert_terms(): return jnp.dot(hidden, down_matrix, preferred_element_type=jnp.float32)  16 us
    all_gather x1, blocking collectives, local(): older_rot = lax.all_gather(cache_rope[0], 'seq', axis=1, tiled=True)  12.7 us
    all_to_all x1, starting transfers between devices, local(): lax.all_to_all(summed, 'ep', split_axis=0, concat_axis=0, tiled=True)  9.67 us
    all_to_all x1, starting transfers between devices, local(): lax.all_to_all(layer_own, 'seq', split_axis=1, concat_axis=0, tiled=True)  8.91 us
  transfers between devices with their start and end apart: 6, of which 5 were waited for; matrix products, arithmetic and copies ran while one was open for 3% of the time, Pallas kernels for 0%

commit v1 on v0

--- a/solution.py
+++ b/solution.py
@@ -115,7 +115,7 @@
     rope_part = lax.dot_general(
         layer, w_rope, (((1,), (1,)), ((), ())), preferred_element_type=jnp.float32
     )
-    raw = lax.psum(jnp.concatenate([latent_part, rope_part], axis=1), "seq")
+    raw = jnp.sum(lax.all_gather(jnp.concatenate([latent_part, rope_part], axis=1), "seq"), axis=0)
     fresh_lat = rms_rows(raw[:, :lat_width], latent_gain).astype(jnp.bfloat16)
     positions = prefix + jnp.arange(new, dtype=jnp.int32)
     fresh_rot = rotate_pairs(raw[:, lat_width:], positions).astype(jnp.bfloat16)

time: 292 us -> 258 us (0.88)
  waiting for transfers between devices: 159 us -> 105 us
  blocking collectives: 46.3 us -> 61.2 us
    psum x1 -> x0, waiting for transfers between devices: 53.4 us -> none  [local(): raw = lax.psum(jnp.concatenate([latent_part, rope_part], axis=1), 'seq')]
    all_gather x0 -> x1, blocking collectives: none -> 14.9 us  [local(): lax.all_gather(jnp.concatenate([latent_part, rope_part], axis=1), 'seq')]
  transfers between devices with their start and end apart: 6 -> 5, of which waited for: 5 -> 4; matrix products, arithmetic and copies ran while one was open for 3% -> 4% of each run, Pallas kernels for 0% -> 0%
where the time goes in v1:
time: 258 us; the launch traced here: 257 us
  waiting for transfers between devices  105 us (41%)
  blocking collectives  61.2 us (24%)
  matrix products  36.9 us (14%)
  starting transfers between devices  18.9 us (7%)
  between operations  14.6 us (6%)
  local copies, waits for them, and re-layouts  13.7 us (5%)
  other arithmetic  7.11 us (3%)
    all_gather x1, waiting for transfers between devices, local(): lax.all_gather(arrived.reshape(total_slots, width), 'seq', axis=0, tiled=...  49.3 us
    reduce_scatter x1, waiting for transfers between devices, local(): summed = lax.psum_scatter(terms, 'seq', scatter_dimension=0, tiled=True)  48.5 us
    all_to_all x1, blocking collectives, local(): lax.all_to_all(outgoing, 'ep', split_axis=0, concat_axis=0, tiled=True)  33.6 us
    dot_general x1, matrix products, expert_terms(): return jnp.dot(hidden, down_matrix, preferred_element_type=jnp.float32)  16 us
    all_gather x1, blocking collectives, local(): lax.all_gather(jnp.concatenate([latent_part, rope_part], axis=1), 'seq')  14.9 us
    all_gather x1, blocking collectives, local(): older_rot = lax.all_gather(cache_rope[0], 'seq', axis=1, tiled=True)  12.7 us
    all_to_all x1, starting transfers between devices, local(): lax.all_to_all(summed, 'ep', split_axis=0, concat_axis=0, tiled=True)  9.83 us
    all_to_all x1, starting transfers between devices, local(): lax.all_to_all(layer_own, 'seq', split_axis=1, concat_axis=0, tiled=True)  8.9 us
  transfers between devices with their start and end apart: 5, of which 4 were waited for; matrix products, arithmetic and copies ran while one was open for 4% of the time, Pallas kernels for 0%

profile of v1, /device:TPU:1, one launch (start us, length us, event | category | flops | bytes accessed | tf_op | source)
XLA Modules:
  0.0 257.4 jit_solution(13368815401783098199)
XLA Ops:
  7.2 0.0 copy-start
  7.2 0.0 all-gather.6.cloned.1.call-start
  7.2 0.8 constant_dynamic-slice_fusion.1
  8.1 0.1 copy.23
  8.2 0.4 compare_reduce_fusion
  8.6 0.1 convert_reduce_fusion
  8.7 0.1 fusion.47
  8.8 1.0 fusion.28
  9.8 1.3 convolution_convert_fusion.1
  11.1 0.3 reshape.118
  11.4 33.6 %all_to_all.29 = bf16[32,2,7168]{2,1,0:T(2,128)(2,1)S(1)} all-to-all(bf16[32,2,7168]{2,1,0:T(2,128)(2,1)S(1)} %reshape.118), channel_id=1, replica_groups=mesh['seq'=8,'ep'=32] {'ep'}, dimensions={0} | all-to-all | bytes 1835008 | tf_op jit(solution)/shard_map/all_to_all | solution.py:88
  45.0 1.3 reshape.119
  46.3 0.0 all-gather.6.cloned.1.call-update
  46.3 0.0 reduce-scatter.2.cloned.1.call-start
  46.4 49.3 %all-gather.6.cloned.1.call-done = bf16[512,7168]{1,0:T(8,128)(2,1)} async-done(((bf16[64,7168]{1,0:T(8,128)(2,1)}), bf16[512,7168]{1,0:T(8,128)(2,1)}) %all-gather.6.cloned.1.call-update) | async-done | bytes 7340048 | tf_op jit(solution)/shard_map/all_gather | solution.py:89
  95.7 6.2 %fusion.4 = f32[512,256]{1,0:T(8,128)S(1)} fusion(bf16[512,7168]{1,0:T(8,128)(2,1)} %all-gather.6.cloned.1.call-done, bf16[1,7168,256]{2,1,0:T(8,128)(2,1)} %param.19), kind=kOutput, calls=%fused_computation.7 | convolution fusion | flops 1879048192 | bytes 11534336 | tf_op jit(solution)/shard_map/dot_general | solution.py:44
  101.9 16.0 %convolution_convert_fusion = bf16[512,7168]{1,0:T(8,128)(2,1)} fusion(bf16[1,256,7168]{2,1,0:T(8,128)(2,1)} %param.21, bf16[512,7168]{1,0:T(8,128)(2,1)} %all-gather.6.cloned.1.call-done, bf16[1,7168,256]{2,1,0:T(8,128)(2,1)} %param.20, f32[512,256]{1,0:T(8,128)S(1)} %fusion.4), kind=kOutput, calls=%fused_computation | convolution fusion | flops 3762552832 | bytes 22544384 | tf_op jit(solution)/shard_map/dot_general | solution.py:47
  117.8 0.0 reduce-scatter.2.cloned.1.call-update
  117.9 0.0 copy-start.6
  117.9 0.0 copy-start.4
  117.9 0.0 copy-start.3
  117.9 0.0 copy-start.5
  117.9 0.0 all-gather.8.cloned.1.call-start
  118.0 0.7 all-gather.8.cloned.1.call-update
  118.7 48.5 %reduce-scatter.2.cloned.1.call-done = bf16[64,7168]{1,0:T(8,128)(2,1)} async-done(((bf16[512,7168]{1,0:T(8,128)(2,1)}), bf16[64,7168]{1,0:T(8,128)(2,1)}) %reduce-scatter.2.cloned.1.call-update) | async-done | bytes 917520 | tf_op jit(solution)/shard_map/reduce_scatter | solution.py:104
  167.2 3.1 %reshape.120 = bf16[32,2,7168]{2,1,0:T(2,128)(2,1)} reshape(bf16[64,7168]{1,0:T(8,128)(2,1)} %reduce-scatter.2.cloned.1.call-done) | data formatting | bytes 1835008 | tf_op jit(solution)/shard_map/reshape | solution.py:105
  170.2 9.8 %all-to-all-start.1 = ((bf16[32,2,7168]{2,1,0:T(2,128)(2,1)}), bf16[32,2,7168]{2,1,0:T(2,128)(2,1)}, u32[]{:S(2)}, u32[]{:S(2)}) async-start(bf16[32,2,7168]{2,1,0:T(2,128)(2,1)} %reshape.120), calls=%async_computation.2 | async-start | bytes 1835008 | tf_op jit(solution)/shard_map/all_to_all | solution.py:106
  180.1 0.0 copy-done.6
  180.1 0.1 constant_dynamic-slice_fusion
  180.2 0.1 copy.24
  180.3 0.0 copy-done.4
  180.3 0.2 reshape_squeeze.7
  180.4 0.0 copy-done.3
  180.4 0.0 copy-start.1
  180.4 0.4 reshape_squeeze.6
  181.5 0.0 copy-done.5
  181.5 12.7 %all-gather.1 = bf16[1,64,1024]{2,1,0:T(8,128)(2,1)S(1)} all-gather(bf16[1,64,128]{2,1,0:T(8,128)(2,1)S(1)} %copy-done.5), channel_id=3, replica_groups=mesh['seq'=8,'ep'=32] {'seq'}, dimensions={2}, use_global_device_ids=true | all-gather | bytes 147456 | tf_op jit(solution)/shard_map/all_gather | solution.py:91
  194.2 0.5 negate_power_fusion
  194.8 0.5 add_convert_fusion
  195.3 0.1 select_reduce_fusion
  195.4 1.8 fusion.26
  197.2 0.0 copy-done.1
  197.2 2.8 %fusion.58 = (f32[512]{0:T(512)S(1)}, f32[512,1024]{1,0:T(8,128)S(1)}) fusion(f32[512,1024]{1,0:T(8,128)} %fusion.26, bf16[512,512]{1,0:T(8,128)(2,1)S(1)} %reshape_squeeze.6, bf16[1,1024,512]{2,1,0:T(8,128)(2,1)} %all-gather.8.cloned.1.call-done, pred[1024]{0:T(1024)(128)(4,1)S(1)} %iota_compare_fusion.2), kind=kOutput, calls=%fused_computation.85 | convolution fusion | flops 538967552 | bytes 5770240 | tf_op jit(solution)/shard_map/dot_general | solution.py:30
  200.0 2.0 all-to-all-done.1
  201.9 3.2 %reshape.121 = bf16[64,7168]{1,0:T(8,128)(2,1)} reshape(bf16[32,2,7168]{2,1,0:T(2,128)(2,1)} %all-to-all-done.1) | data formatting | bytes 1835008 | tf_op jit(solution)/shard_map/reshape | solution.py:109
  205.1 2.3 fusion
  207.4 8.9 %all-to-all-start.2 = ((bf16[4,8,896]{2,0,1:T(4,128)(2,1)}), bf16[4,8,896]{2,0,1:T(4,128)(2,1)}, u32[]{:S(2)}, u32[]{:S(2)}) async-start(bf16[4,8,896]{2,0,1:T(4,128)(2,1)} %bitcast.60), calls=%async_computation.3 | async-start | bytes 114688 | tf_op jit(solution)/shard_map/all_to_all | solution.py:113
  216.3 0.5 fusion.6
  216.8 4.5 %all-to-all-done.2 = bf16[4,8,896]{2,0,1:T(4,128)(2,1)} async-done(((bf16[4,8,896]{2,0,1:T(4,128)(2,1)}), bf16[4,8,896]{2,0,1:T(4,128)(2,1)}, u32[]{:S(2)}, u32[]{:S(2)}) %all-to-all-start.2) | async-done | bytes 57376 | tf_op jit(solution)/shard_map/all_to_all | solution.py:113
  221.3 1.5 broadcast_in_dim.34
  222.7 1.5 all_to_all.25
  224.2 1.1 fusion.61
  225.3 0.0 copy-done
  225.3 1.1 fusion.60
  226.4 14.9 %all-gather.2 = f32[256,576]{1,0:T(8,128)} all-gather(f32[32,576]{1,0:T(8,128)S(1)} %pad_maximum_fusion), channel_id=4, replica_groups=mesh['seq'=8,'ep'=32] {'seq'}, dimensions={0}, use_global_device_ids=true | all-gather | bytes 663552 | tf_op jit(solution)/shard_map/all_gather | solution.py:118
  241.3 1.8 reduce_sum.66
  243.1 1.0 multiply_reduce_fusion
  244.1 0.0 copy-done.7
  244.1 1.1 fusion.57
  245.2 1.0 fusion.44
  246.1 1.1 fusion.59
  247.3 2.0 convolution_multiply_fusion
  249.3 0.3 fusion.9
  249.7 1.2 broadcast_in_dim_reshape.3
  (14 shorter events, 0.1 us)
Async XLA Ops:
  7.2 218.1 %copy-start = (bf16[896,512]{1,0:T(8,128)(2,1)S(1)}, bf16[896,512]{1,0:T(8,128)(2,1)}, u32[]{:S(2)}) copy-start(bf16[896,512]{1,0:T(8,128)(2,1)} %param.22) | copy-start | bytes 2752516
  7.2 88.5 %all-gather.6.cloned.1.call-start = ((), (), s32[]{:S(2)}) async-start(), calls=%async_computation.4 | async-start | bytes 8257536 | tf_op jit(solution)/shard_map/all_gather | solution.py:89
  46.3 120.8 %reduce-scatter.2.cloned.1.call-start = ((), (), s32[]{:S(2)}) async-start(), calls=%async_computation.5 | async-start | bytes 8257536 | tf_op jit(solution)/shard_map/reduce_scatter | solution.py:104
  117.9 62.2 %copy-start.6 = (f32[1,32,8]{1,2,0:T(8,128)S(1)}, f32[1,32,8]{1,2,0:T(8,128)}, u32[]{:S(2)}) copy-start(f32[1,32,8]{1,2,0:T(8,128)} %param.18) | copy-start | bytes 3076
  117.9 62.4 %copy-start.4 = (bf16[1,4,8192]{2,1,0:T(4,128)(2,1)S(1)}, bf16[1,4,8192]{2,1,0:T(4,128)(2,1)}, u32[]{:S(2)}) copy-start(bf16[1,4,8192]{2,1,0:T(4,128)(2,1)} %param.29) | copy-start | bytes 196612
  117.9 62.5 %copy-start.3 = (bf16[1,4,65536]{2,1,0:T(4,128)(2,1)S(1)}, bf16[1,4,65536]{2,1,0:T(4,128)(2,1)}, u32[]{:S(2)}) copy-start(bf16[1,4,65536]{2,1,0:T(4,128)(2,1)} %param.28) | copy-start | bytes 1572868
  117.9 63.6 %copy-start.5 = (bf16[1,64,128]{2,1,0:T(8,128)(2,1)S(1)}, bf16[1,64,128]{2,1,0:T(8,128)(2,1)}, u32[]{:S(2)}) copy-start(bf16[1,64,128]{2,1,0:T(8,128)(2,1)} %param.27) | copy-start | bytes 49156
  117.9 79.3 %all-gather.8.cloned.1.call-start = ((), (), s32[]{:S(2)}) async-start(), calls=%async_computation.6 | async-start | bytes 1179648 | tf_op jit(solution)/shard_map/all_gather | solution.py:90
  170.2 31.7 %all-to-all-start.1 = ((bf16[32,2,7168]{2,1,0:T(2,128)(2,1)}), bf16[32,2,7168]{2,1,0:T(2,128)(2,1)}, u32[]{:S(2)}, u32[]{:S(2)}) async-start(bf16[32,2,7168]{2,1,0:T(2,128)(2,1)} %reshape.120), calls=%async_computation.2 | async-start | bytes 1835008 | tf_op jit(solution)/shard_map/all_to_all | solution.py:106
  180.4 16.7 %copy-start.1 = (bf16[512,64]{1,0:T(8,128)(2,1)}, bf16[512,64]{1,0:T(8,128)(2,1)S(1)}, u32[]{:S(2)}) copy-start(bf16[512,64]{1,0:T(8,128)(2,1)S(1)} %reshape_squeeze.7) | copy-start | bytes 196612
  205.1 39.0 %copy-start.7 = (f32[512]{0:T(512)S(1)}, f32[512]{0:T(512)}, u32[]{:S(2)}) copy-start(f32[512]{0:T(512)} %param.24) | copy-start | bytes 6148
  207.4 13.8 %all-to-all-start.2 = ((bf16[4,8,896]{2,0,1:T(4,128)(2,1)}), bf16[4,8,896]{2,0,1:T(4,128)(2,1)}, u32[]{:S(2)}, u32[]{:S(2)}) async-start(bf16[4,8,896]{2,0,1:T(4,128)(2,1)} %bitcast.60), calls=%async_computation.3 | async-start | bytes 114688 | tf_op jit(solution)/shard_map/all_to_all | solution.py:113
  243.1 6.3 %copy-start.2 = (f32[32,576]{1,0:T(8,128)S(1)}, f32[32,576]{1,0:T(8,128)}, u32[]{:S(2)}) copy-start(f32[32,576]{1,0:T(8,128)} %reduce_sum.66) | copy-start | bytes 221188
Sparse Core Ops, SparseCore 0:
  46.5 49.1 all-gather.5
  118.0 49.1 reduce-scatter.1
  169.0 26.7 all-gather.7
